TPU v7x, 512 devices: a whole 4x8x8 slice. The times are simulated.
512 devices in a mesh: frame: 32 (over z, y_lo, core), orient: 4 (over x), pix: 4 (over y_hi).
Axes of the slice: x: 4, y: 8 (y_hi: 4, y_lo: 2; y = y_hi * 2 + y_lo), z: 8, core: 2. Of those that a mesh axis runs over, the one named last changes fastest.
Arguments:
- photon_counts: int32 [512, 16384], P('frame', 'pix'), may hold values from 0 to 8, as said below
- slices: bfloat16 [768, 16384], P('orient', 'pix'), may hold values from 0.049804688 to 2
- owner_ids: int32 [768, 128], P('orient', 'pix'), may hold values from 0 to 3
- tile_ids: int32 [768, 128], P('orient', 'pix'), may hold values from 0 to 2047
- patch_count: int32 [768], P('orient'), may hold values from 16 to 128
- old_model: float32 [1024, 128], P(('frame', 'orient', 'pix')), may hold values from 0.1 to 2
Outputs:
- orient_prob: bfloat16 [512, 768], P('frame', 'orient')
- merged: float32 [1024, 128], P(('frame', 'orient', 'pix'))
Inputs may be any that keep to these rules, and one draw needn't show every extreme that they name: `photon_counts`: each frame's counts stay below a level of 3 to 9 drawn for that frame.
All inputs are finite; a program needn't handle non-finite values.
Results may differ from a plain program's by a relative error of at most 0.0029.
The roundings to bfloat16 on the way count: a program that leaves them out, or rounds other values in their place, can miss the bound.
Values sent between devices are 32-bit elements; how exact they have to be, the bound alone decides.
A program may use at most 64 MiB of HBM per device.

v0:
```python
import math

import jax
import jax.numpy as jnp
from jax import lax
from jax.sharding import PartitionSpec as P

P_SIZE = 16384
NB = 4
BRICK_ROWS = 256
SHIFTS = 8


def sent_to_all(shard, axis):
    devices = lax.axis_size(axis)
    return lax.all_to_all(
        jnp.broadcast_to(shard[None], (devices, *shard.shape)), axis, 0, 0, tiled=True
    )


def of_everyone(shard, axis):
    everything = sent_to_all(shard, axis)
    return jnp.sum(everything, axis=0)


def in_one(arrays, axis):
    line, at, done = (jnp.concatenate([a.reshape(-1) for a in arrays]), 0, [])
    subtotal = of_everyone(line, axis)
    for a in arrays:
        done.append(subtotal[at : at + a.size].reshape(a.shape))
        at += a.size
    return tuple(done)


def gathered_once(shard, axis):
    leaves = jax.tree.leaves(shard)
    sequence = sorted(range(len(leaves)), key=lambda k: -leaves[k].size)
    width = (1, *leaves[sequence[0]].shape)[-1]
    lines = [
        jnp.pad(leaves[k].reshape(-1), (0, -leaves[k].size % width)).reshape(-1, width)
        for k in sequence
    ]
    both, at, found = (sent_to_all(jnp.concatenate(lines), axis), 0, {})
    for k, line in zip(sequence, lines):
        share = both[:, at : at + len(line)].reshape(len(both), -1)
        found[k] = share[:, : leaves[k].size].reshape(-1, *leaves[k].shape)
        at += len(line)
    numbers = iter(range(len(leaves)))
    return jax.tree.map(lambda _: found[next(numbers)], shard)


def combined_pairwise(pieces, combine):
    while len(jax.tree.leaves(pieces)[0]) > 1:
        pieces = jax.vmap(combine)(
            *(jax.tree.map(lambda part: part[side::2], pieces) for side in (0, 1))
        )
    return jax.tree.map(lambda part: part[0], pieces)


def combined_all(shard, axis, combine):
    pieces = gathered_once(shard, axis)
    return combined_pairwise(pieces, combine)


def deposit(values, weights, owners, tile_ids, live_mask, rows_total):
    shift_ids = tile_ids % SHIFTS
    inner_rows = tile_ids // SHIFTS
    moved = jnp.zeros(values.shape, jnp.float32)
    for shift in range(SHIFTS):
        rolled = jnp.roll(values, 17 * shift, axis=2)
        moved = jnp.where((shift_ids == shift)[:, :, None], rolled, moved)
    flat_values = (moved * live_mask[:, :, None]).reshape(-1, 128)
    flat_weights = (live_mask * weights[:, None]).reshape(-1, 1)
    flat_owners = owners.reshape(-1)
    flat_inner = inner_rows.reshape(-1)
    brick_lines = lax.iota(jnp.int32, BRICK_ROWS)

    def one_brick(brick):
        picked = (flat_inner[None, :] == brick_lines[:, None]) & (flat_owners[None, :] == brick)
        onehot = picked.astype(jnp.float32)
        summed = jnp.dot(
            onehot, flat_values, precision=lax.Precision.HIGHEST, preferred_element_type=jnp.float32
        )
        weighed = jnp.dot(
            onehot,
            flat_weights,
            precision=lax.Precision.HIGHEST,
            preferred_element_type=jnp.float32,
        )
        return (summed, weighed[:, 0])

    brick_sum, brick_weight = lax.map(one_brick, lax.iota(jnp.int32, rows_total // BRICK_ROWS))
    return (brick_sum.reshape(rows_total, 128), brick_weight.reshape(rows_total))


def combine_stats(earlier, latter):
    score_top = jnp.maximum(earlier[0], latter[0])
    summed = earlier[1] * jnp.exp(earlier[0] - score_top) + latter[1] * jnp.exp(
        latter[0] - score_top
    )
    return (score_top, summed)


def shards(photon_counts, slices, owner_ids, tile_ids, patch_count, old_model):
    orient_rows = slices.shape[0]
    pixel_cols = slices.shape[1]
    local_patches = pixel_cols // 128
    rows_total = NB * BRICK_ROWS
    frames_bf = photon_counts.astype(jnp.bfloat16)
    log_slice = jnp.log(slices.astype(jnp.float32)).astype(jnp.bfloat16)
    fit_part = jnp.einsum("fp,rp->fr", frames_bf, log_slice, preferred_element_type=jnp.float32)
    mass_part = jnp.sum(slices, axis=1, dtype=jnp.float32)
    fit, slice_mass = in_one((fit_part, mass_part), "pix")
    score = (fit - slice_mass[None, :]) * (1.0 / math.sqrt(P_SIZE))
    local_top = jnp.max(score, axis=1)
    local_total = jnp.sum(jnp.exp(score - local_top[:, None]), axis=1)
    score_top, score_total = combined_all((local_top, local_total), "orient", combine_stats)
    weights_exp = jnp.exp(score - score_top[:, None])
    orient_prob = (weights_exp / score_total[:, None]).astype(jnp.bfloat16)
    weight_part = jnp.sum(orient_prob.astype(jnp.float32), axis=0)
    photon_part = jnp.einsum(
        "fr,fp->rp", orient_prob, frames_bf, preferred_element_type=jnp.float32
    )
    pix_start = lax.axis_index("pix") * local_patches
    patch_id = pix_start + lax.iota(jnp.int32, local_patches)
    live_mask = (patch_id[None, :] < patch_count[:, None]).astype(jnp.float32)
    brick_part, weight_rows = deposit(
        photon_part.reshape(orient_rows, local_patches, 128),
        weight_part,
        owner_ids,
        tile_ids,
        live_mask,
        rows_total,
    )
    brick_sum, brick_weight = (
        lax.psum_scatter(brick_part, ("frame", "orient", "pix"), scatter_dimension=0, tiled=True),
        lax.psum_scatter(weight_rows, ("frame", "orient", "pix"), scatter_dimension=0, tiled=True),
    )
    frames_total = photon_counts.shape[0] * lax.axis_size("frame")
    patches_total = pixel_cols * lax.axis_size("pix") // 128
    prior = frames_total * patches_total / (4.0 * rows_total)
    merged = (brick_sum + prior * old_model) / (brick_weight[:, None] + prior)
    return (orient_prob, merged)


def solution(mesh):
    placed = (
        P("frame", "pix"),
        P("orient", "pix"),
        P("orient", "pix"),
        P("orient", "pix"),
        P("orient"),
        P(("frame", "orient", "pix"), None),
    )
    return jax.shard_map(
        shards,
        mesh=mesh,
        in_specs=placed,
        out_specs=(P("frame", "orient"), P(("frame", "orient", "pix"), None)),
        check_vma=False,
    )
```

profile of v0, /device:TPU:1, one launch (start us, length us, event | category | flops | bytes accessed | tf_op | source)
XLA Modules:
  0.0 373.4 jit_solution(17174908706387698518)
XLA Ops:
  7.2 1.7 convert_reduce_fusion
  8.9 2.0 fusion.21
  11.7 7.6 %all-to-all-start = ((f32[4,1,3264]{2,1,0:T(1,128)}), f32[4,1,3264]{2,1,0:T(1,128)S(1)}, u32[]{:S(2)}, u32[]{:S(2)}) async-start(f32[4,1,3264]{2,1,0:T(1,128)} %broadcast_in_dim.88), calls=%async_computation | async-start | bytes 106496 | tf_op jit(solution)/shard_map/all_to_all | solution.py:16
  19.5 6.7 %all-to-all-done = f32[4,1,3264]{2,1,0:T(1,128)S(1)} async-done(((f32[4,1,3264]{2,1,0:T(1,128)}), f32[4,1,3264]{2,1,0:T(1,128)S(1)}, u32[]{:S(2)}, u32[]{:S(2)}) %all-to-all-start) | async-done | bytes 52256 | tf_op jit(solution)/shard_map/all_to_all | solution.py:16
  27.3 4.0 %all-to-all-start.1 = ((f32[4,2,16]{2,1,0:T(2,128)}), f32[4,2,16]{2,1,0:T(2,128)S(1)}, u32[]{:S(2)}, u32[]{:S(2)}) async-start(f32[4,2,16]{2,1,0:T(2,128)} %broadcast_in_dim.89), calls=%async_computation.1 | async-start | bytes 8192 | tf_op jit(solution)/shard_map/all_to_all | solution.py:16
  32.2 3.2 all-to-all-done.1
  38.1 0.9 slice.142
  38.9 0.9 slice.144
  39.8 0.9 slice.146
  40.7 0.9 slice.148
  42.5 14.9 %fusion.20 = f32[192,32,128]{2,0,1:T(8,128)S(1)} fusion(f32[192,32,9]{2,0,1:T(8,128)S(1)} %bitcast.50, f32[192,32,119]{2,0,1:T(8,128)S(1)} %slice.138, f32[192,32,26]{2,0,1:T(8,128)S(1)} %bitcast.51, f32[192,32,102]{2,0,1:T(8,128)S(1)} %slice.140, f32[192,32,43]{2,0,1:T(8,128)S(1)} %bitcast.52, f32[192,32,85]{2,0,1:T(8,128)S(1)} %slice.142, ...), kind=kLoop, calls=%fused_computation.18 | loop fusion | flops 12582912 | bytes 28385280 | tf_op jit(solution)/shard_map/mul | solution.py:72
  57.4 1.8 copy.84
  59.2 35.3 %while.14 = (s32[]{:T(128)}, f32[4,256,128]{2,1,0:T(8,128)}, f32[4,256]{1,0:T(4,128)S(1)}, s32[192,32]{1,0:T(8,128)}, s32[4]{0:T(128)S(1)}, /*index=5*/s32[192,3...) while((s32[]{:T(128)}, f32[4,256,128]{2,1,0:T(8,128)}, ...), condition=%wide.wide.region_6.7_spmd.clone, body=%wide.wide.region_5.6_spmd.clone.sunk | while | flops 2441103360 | bytes 3484945 | solution.py:92
  60.7 3.1 fusion.52
  63.8 4.2 %fusion.51 = f32[4,256,128]{2,1,0:T(8,128)} fusion(f32[4,256,128]{2,1,0:T(8,128)} %get-tuple-element.287, s32[]{:T(128)} %get-tuple-element.286, f32[6144,128]{1,0:T(8,128)S(1)} %get-tuple-element.305, s32[6144]{0:T(1024)S(1)} %get-tuple-element.309, pred[6144]{0:T(1024)(128)(4,1)S(1)} %eq.147), kind=kOutput, calls=%fused_computation.11.clone.clone.1 | convolution fusion | flops 2419064832 | bytes 3308032 | tf_op jit(solution)/shard_map/while/body/eval_jaxpr/dot_general | solution.py:81
  69.6 3.1 fusion.52
  72.7 4.2 %fusion.51 = f32[4,256,128]{2,1,0:T(8,128)} fusion(f32[4,256,128]{2,1,0:T(8,128)} %get-tuple-element.287, s32[]{:T(128)} %get-tuple-element.286, f32[6144,128]{1,0:T(8,128)S(1)} %get-tuple-element.305, s32[6144]{0:T(1024)S(1)} %get-tuple-element.309, pred[6144]{0:T(1024)(128)(4,1)S(1)} %eq.147), kind=kOutput, calls=%fused_computation.11.clone.clone.1 | convolution fusion | flops 2419064832 | bytes 3308032 | tf_op jit(solution)/shard_map/while/body/eval_jaxpr/dot_general | solution.py:81
  78.4 3.1 fusion.52
  81.5 4.2 %fusion.51 = f32[4,256,128]{2,1,0:T(8,128)} fusion(f32[4,256,128]{2,1,0:T(8,128)} %get-tuple-element.287, s32[]{:T(128)} %get-tuple-element.286, f32[6144,128]{1,0:T(8,128)S(1)} %get-tuple-element.305, s32[6144]{0:T(1024)S(1)} %get-tuple-element.309, pred[6144]{0:T(1024)(128)(4,1)S(1)} %eq.147), kind=kOutput, calls=%fused_computation.11.clone.clone.1 | convolution fusion | flops 2419064832 | bytes 3308032 | tf_op jit(solution)/shard_map/while/body/eval_jaxpr/dot_general | solution.py:81
  87.2 3.1 fusion.52
  90.3 4.2 %fusion.51 = f32[4,256,128]{2,1,0:T(8,128)} fusion(f32[4,256,128]{2,1,0:T(8,128)} %get-tuple-element.287, s32[]{:T(128)} %get-tuple-element.286, f32[6144,128]{1,0:T(8,128)S(1)} %get-tuple-element.305, s32[6144]{0:T(1024)S(1)} %get-tuple-element.309, pred[6144]{0:T(1024)(128)(4,1)S(1)} %eq.147), kind=kOutput, calls=%fused_computation.11.clone.clone.1 | convolution fusion | flops 2419064832 | bytes 3308032 | tf_op jit(solution)/shard_map/while/body/eval_jaxpr/dot_general | solution.py:81
  94.6 105.4 %all-reduce.1 = f32[1024]{0:T(1024)S(1)} all-reduce(f32[1024]{0:T(1024)S(1)} %bitcast.59), channel_id=3, replica_groups=mesh['frame'=32,'orient'=4,'pix'=4] {'frame','orient','pix'}, use_global_device_ids=true, to_apply=%region_8.9.clone | all-reduce | flops 1024 | bytes 8192
  200.0 165.2 %all-reduce.4.cloned.1.call-done = f32[1024,128]{1,0:T(8,128)} async-done(((f32[1024,128]{1,0:T(8,128)}), f32[1024,128]{1,0:T(8,128)}) %all-reduce.4.cloned.1.call-update) | async-done | bytes 524304
  365.2 1.3 fusion.31
  (75 shorter events, 12.5 us)
Async XLA Ops:
  7.2 28.5 %copy-start = (s32[16,4096]{1,0:T(8,128)S(1)}, s32[16,4096]{1,0:T(8,128)}, u32[]{:S(2)}) copy-start(s32[16,4096]{1,0:T(8,128)} %param.8) | copy-start | bytes 786436
  7.2 12.2 %copy-start.2 = (s32[192,32]{0,1:T(8,128)S(1)}, s32[192,32]{0,1:T(8,128)}, u32[]{:S(2)}) copy-start(s32[192,32]{0,1:T(8,128)} %param.11) | copy-start | bytes 73732
  7.2 12.2 %copy-start.3 = (s32[192]{0:T(256)S(1)}, s32[192]{0:T(256)}, u32[]{:S(2)}) copy-start(s32[192]{0:T(256)} %param.12) | copy-start | bytes 2308
  7.2 24.9 %copy-start.5 = (s32[192,32]{0,1:T(8,128)S(1)}, s32[192,32]{0,1:T(8,128)}, u32[]{:S(2)}) copy-start(s32[192,32]{0,1:T(8,128)} %param.10) | copy-start | bytes 73732
  11.7 14.5 %all-to-all-start = ((f32[4,1,3264]{2,1,0:T(1,128)}), f32[4,1,3264]{2,1,0:T(1,128)S(1)}, u32[]{:S(2)}, u32[]{:S(2)}) async-start(f32[4,1,3264]{2,1,0:T(1,128)} %broadcast_in_dim.88), calls=%async_computation | async-start | bytes 106496 | tf_op jit(solution)/shard_map/all_to_all | solution.py:16
  27.3 8.2 %all-to-all-start.1 = ((f32[4,2,16]{2,1,0:T(2,128)}), f32[4,2,16]{2,1,0:T(2,128)S(1)}, u32[]{:S(2)}, u32[]{:S(2)}) async-start(f32[4,2,16]{2,1,0:T(2,128)} %broadcast_in_dim.89), calls=%async_computation.1 | async-start | bytes 8192 | tf_op jit(solution)/shard_map/all_to_all | solution.py:16
  31.3 333.9 %all-reduce.4.cloned.1.call-start = ((), (), s32[]{:S(2)}) async-start(), calls=%async_computation.2 | async-start | bytes 1048576
  31.4 0.6 copy-start.1
  35.7 1.5 copy-start.4
  59.2 306.0 %copy-start.6 = (f32[2,128]{1,0:T(2,128)S(1)}, f32[2,128]{1,0:T(2,128)}, u32[]{:S(2)}) copy-start(f32[2,128]{1,0:T(2,128)} %param.13) | copy-start | bytes 3076
Sparse Core Ops, SparseCore 0:
  94.7 270.5 all-reduce.3
where the time goes:
time: 374 us; the launch traced here: 373 us
  waiting for transfers between devices  175 us (47%)
  blocking collectives  105 us (28%)
  matrix products  31.7 us (8%)
  other arithmetic  21.5 us (6%)
  between operations  14.2 us (4%)
  local copies, waits for them, and re-layouts  13.7 us (4%)
  starting transfers between devices  11.7 us (3%)
    unnamed x2, waiting for transfers between devices  165 us
    unnamed x1, blocking collectives  105 us
    dot_general x4, matrix products, one_brick(): jnp.dot(onehot, flat_values, precision=lax.Precision.HIGHEST, preferred_e...  16.9 us
    mul x1, other arithmetic, deposit(): flat_values = (moved * live_mask[:, :, None]).reshape(-1, 128)  14.9 us
    dot_general x4, matrix products, one_brick(): jnp.dot(onehot, flat_weights, precision=lax.Precision.HIGHEST, preferred_...  12.2 us
    all_to_all x2, starting transfers between devices, sent_to_all(): lax.all_to_all(jnp.broadcast_to(shard[None], (devices, *shard.shape)), ax...  11.7 us
    all_to_all x2, waiting for transfers between devices, sent_to_all(): lax.all_to_all(jnp.broadcast_to(shard[None], (devices, *shard.shape)), ax...  9.87 us
  transfers between devices with their start and end apart: 3, of which 3 were waited for; matrix products, arithmetic and copies ran while one was open for 0% of the time, Pallas kernels for 0%

commit v1 on v0

v1 whole, which is shorter than its diff:
```python
import functools
import math

import jax
import jax.numpy as jnp
from jax import lax
from jax.experimental import pallas as pl
from jax.experimental.pallas import tpu as pltpu
from jax.sharding import PartitionSpec as P

XN, YN, ZN = 4, 8, 8
PEERS_X = XN - 1
PIXELS = 16384
SHIFTS = 8
PRIOR = 512 * 128 / (4.0 * 1024)
ROWS = 512
KTOT = 192 * 32
F32 = jnp.float32
BF16 = jnp.bfloat16
NT = (((1,), (1,)), ((), ()))


def lanes(shape):
    return lax.broadcasted_iota(jnp.int32, shape, len(shape) - 1)


def sublanes(shape):
    return lax.broadcasted_iota(jnp.int32, shape, len(shape) - 2)


def kernel(
    counts_in, slices_in, owner_in, tile_in, count_in, old_in,
    prob_out, merged_out,
    cnt, pcnt, sl, own_v, til_v, pc_v, old_v,
    idpad, fit_scr, shm_scr, rep_scr, wsel_scr, grolled, rowk, ohs, rhs,
    psend, precv, ssend, srecv, ppart,
    xs, xr, asd, ar, bsd, br,
    loc_sem, fr_send, fr_recv, p_send, p_recv, s_send, s_recv, x_send, x_recv, a_send, a_recv, b_send, b_recv,
):
    fi = lax.axis_index("frame")
    x = lax.axis_index("orient")
    y_hi = lax.axis_index("pix")
    z = fi // 4
    y_lo = (fi // 2) % 2
    core = fi % 2
    y = y_hi * 2 + y_lo
    swap = 1 - core

    def place(xx, yy, zz, cc):
        return {"frame": zz * 4 + (yy % 2) * 2 + cc, "orient": xx, "pix": yy // 2}

    locals_ = [
        pltpu.make_async_copy(counts_in, cnt, loc_sem.at[0]),
        *[
            pltpu.make_async_copy(
                slices_in.at[:, c * 1024 : (c + 1) * 1024], sl.at[:, c * 1024 : (c + 1) * 1024], loc_sem.at[1 + c]
            )
            for c in range(4)
        ],
        pltpu.make_async_copy(owner_in, own_v, loc_sem.at[5]),
        pltpu.make_async_copy(tile_in, til_v, loc_sem.at[6]),
        pltpu.make_async_copy(count_in, pc_v, loc_sem.at[7]),
        pltpu.make_async_copy(old_in, old_v, loc_sem.at[8]),
    ]
    for copy in locals_:
        copy.start()

    barrier = pltpu.get_barrier_semaphore()
    pl.semaphore_signal(barrier, inc=1, device_id=place(x, y, z, swap))
    for d in range(1, XN):
        for cc in (core, swap):
            pl.semaphore_signal(barrier, inc=1, device_id=place((x + d) % XN, y, z, cc))
    for d in range(1, YN):
        pl.semaphore_signal(barrier, inc=1, device_id=place(x, (y + d) % YN, z, core))
    for d in range(1, ZN):
        pl.semaphore_signal(barrier, inc=1, device_id=place(x, y, (z + d) % ZN, core))

    locals_[0].wait()
    fit = jnp.zeros((16, 192), F32)
    mass = jnp.zeros((192, 128), F32)
    for c in range(16):
        if c % 4 == 0:
            locals_[1 + c // 4].wait()
        s32 = sl[:, c * 256 : (c + 1) * 256].astype(F32)
        mass = mass + (s32[:, :128] + s32[:, 128:])
        fr = cnt[:, c * 256 : (c + 1) * 256].astype(F32).astype(BF16)
        fit = fit + lax.dot_general(fr, jnp.log(s32).astype(BF16), NT, preferred_element_type=F32)
    fit = fit - lax.dot_general(
        jnp.ones((16, 128), F32), mass, NT, precision=lax.Precision.HIGHEST, preferred_element_type=F32
    )
    fit_scr[...] = jnp.zeros((16, 256), F32)
    fit_scr[:, 0:192] = fit
    lane8 = lanes((8, 128))
    psend[0:16, :] = fit_scr[:, 0:128]
    psend[16:24, :] = jnp.where(lane8 < 64, fit_scr[0:8, 128:256], pltpu.roll(fit_scr[8:16, 128:256], 64, 1))

    pl.semaphore_wait(barrier, 1 + 2 * PEERS_X + (YN - 1) + (ZN - 1))

    p_copies = [
        pltpu.make_async_remote_copy(
            psend, precv.at[d - 1], p_send.at[d - 1], p_recv.at[d - 1],
            device_id=place(x, (y + 2 * d) % YN, z, core),
        )
        for d in range(1, 4)
    ]
    for copy in p_copies:
        copy.start()
    swap_frames = pltpu.make_async_remote_copy(
        cnt, pcnt, fr_send.at[0], fr_recv.at[0], device_id=place(x, y, z, swap)
    )
    swap_frames.start()

    for copy in locals_[5:]:
        copy.wait()
    tid = til_v[...]
    rid = own_v[...] * 256 + (tid >> 3)
    ry = ((rid >> 1) & 3) * 2 + ((rid >> 6) & 1)
    rz = rid >> 7
    spot = ((rid >> 3) & 3) * 128 + (ry * swap + rz * core) * 16 + (rz * swap + ry * core) * 2 + (rid & 1)
    spot = jnp.where(((rid >> 5) & 1) == core, spot, -1)
    idpad[...] = jnp.zeros((256, 128), jnp.int32)
    idpad[0:192, 0:32] = spot
    turned = jnp.transpose(idpad[...])
    rowk[0:32, :] = turned[0:32, 0:128]
    rowk[32:48, :] = jnp.where(
        lanes((16, 128)) < 64, turned[0:16, 128:256], pltpu.roll(turned[16:32, 128:256], 64, 1)
    )
    eye = (sublanes((192, 192)) == lanes((192, 192))).astype(F32).astype(BF16)
    pc_col = lax.dot_general(
        eye, jnp.broadcast_to(pc_v[...].astype(F32), (128, 192)).astype(BF16), NT, preferred_element_type=F32
    )
    shm_scr[...] = jnp.full((192, 128), float(SHIFTS), F32)
    live = (lanes((192, 32)) + y_hi * 32).astype(F32) < pc_col[:, 0:32]
    shm_scr[:, 0:32] = jnp.where(live, (tid & 7).astype(F32), float(SHIFTS))

    def roll_frames(source, half):
        def body(q, _):
            tile = source[:, pl.ds(pl.multiple_of(q * 128, 128), 128)].astype(F32)
            for s in range(SHIFTS):
                moved = pltpu.roll(tile, 17 * s, 1) if s else tile
                grolled[q, half * 128 + s * 16 : half * 128 + (s + 1) * 16, :] = moved.astype(BF16)
            return 0

        lax.fori_loop(0, 32, body, 0, unroll=4)

    def onehot(first, last):
        def body(kb, _):
            line = jnp.broadcast_to(rowk[pl.ds(kb, 1), :], (128, 128))
            for b in range(4):
                hit = line == sublanes((128, 128)) + b * 128
                ohs[b * 128 : (b + 1) * 128, pl.ds(pl.multiple_of(kb * 128, 128), 128)] = jnp.where(
                    hit, 1.0, 0.0
                ).astype(BF16)
            return 0

        lax.fori_loop(first, last, body, 0, unroll=2)

    roll_frames(cnt, 0)
    onehot(0, 16)

    for copy in p_copies:
        copy.wait_recv()
    score = (psend[...] + precv[0] + precv[1] + precv[2]) * (1.0 / math.sqrt(PIXELS))
    score_a, tail = score[0:16], score[16:24]
    off = -3.0e38
    score_b = jnp.concatenate(
        [jnp.where(lane8 < 64, tail, off), jnp.where(lane8 < 64, pltpu.roll(tail, 64, 1), off)], axis=0
    )
    top = jnp.maximum(
        jnp.max(score_a, axis=1, keepdims=True), jnp.max(score_b, axis=1, keepdims=True)
    )
    exp_a = jnp.exp(score_a - top)
    exp_b = jnp.exp(score_b - top)
    total = jnp.sum(exp_a, axis=1, keepdims=True) + jnp.sum(exp_b, axis=1, keepdims=True)
    ssend[0:8, :] = jnp.where(
        lane8 < 64,
        jnp.where(lane8 < 32, top[0:8], total[0:8]),
        jnp.where(lane8 < 96, top[8:16], total[8:16]),
    )
    ssend[8:24, :] = exp_a
    ssend[24:32, :] = jnp.where(lane8 < 64, exp_b[0:8], pltpu.roll(exp_b[8:16], 64, 1))
    s_copies = []
    for d in range(1, XN):
        for rel, cc in enumerate((core, swap)):
            slot = (d - 1) * 2 + rel
            s_copies.append(
                pltpu.make_async_remote_copy(
                    ssend.at[0:8], srecv.at[slot], s_send.at[slot], s_recv.at[slot],
                    device_id=place((x + d) % XN, y, z, cc),
                )
            )
    s_copies.append(
        pltpu.make_async_remote_copy(
            ssend, ppart, s_send.at[6], s_recv.at[6], device_id=place(x, y, z, swap)
        )
    )
    for copy in s_copies:
        copy.start()

    swap_frames.wait_recv()
    roll_frames(pcnt, 1)
    onehot(16, 48)

    for copy in s_copies:
        copy.wait_recv()

    def probabilities(packed, others):
        stats = packed[0:8, :]
        every = [stats, *others]
        most = functools.reduce(jnp.maximum, every)
        scale = pltpu.roll(jnp.exp(stats - most), 32, 1)
        whole = stats * scale
        for other in others:
            whole = whole + other * pltpu.roll(jnp.exp(other - most), 32, 1)
        factor = scale / whole
        low, high = factor[:, 32:33], factor[:, 96:97]
        prob_a = jnp.concatenate([packed[8:16, :] * low, packed[16:24, :] * high], axis=0)
        tail = packed[24:32, :]
        prob_b = jnp.concatenate([tail * low, pltpu.roll(tail, 64, 1) * high], axis=0)
        return prob_a.astype(BF16), prob_b.astype(BF16)

    own_a, own_b = probabilities(ssend, [srecv[0], srecv[2], srecv[4]])
    her_a, her_b = probabilities(ppart, [srecv[1], srecv[3], srecv[5]])
    prob_out[:, 0:128] = own_a
    prob_out[:, 128:192] = own_b[:, 0:64]

    stack = jnp.concatenate(
        [
            jnp.concatenate([own_a, own_b], axis=1)] * SHIFTS + [
            jnp.concatenate([her_a, her_b], axis=1)] * SHIFTS,
        axis=0,
    )
    eye = (sublanes((192, 256)) == lanes((192, 256))).astype(F32).astype(BF16)
    rep = lax.dot_general(eye, stack, NT, preferred_element_type=F32)
    rep_scr[...] = rep
    lane_shift = (lanes((192, 256)) % 128) // 16
    weights = jnp.dot(
        jnp.where(lane_shift == 0, rep, 0.0).astype(BF16), jnp.ones((256, 128), BF16), preferred_element_type=F32
    )
    upper = weights.astype(BF16).astype(F32)
    wsel_scr[...] = jnp.where(lanes((192, 128)) < 64, upper, weights - upper)

    def patches(t4, _):
        columns = pltpu.roll(shm_scr[...], 128 - 4 * t4, 1)
        for u in range(4):
            t = t4 * 4 + u
            for h in range(2):
                q = t + 16 * h
                shift = jnp.broadcast_to(columns[:, u + 16 * h : u + 16 * h + 1], (192, 128))
                lane = ((lanes((192, 128)) % 128) // 16).astype(F32)
                same = shift == lane
                left = jnp.concatenate(
                    [
                        jnp.where(same, rep_scr[:, 0:128], 0.0).astype(BF16),
                        jnp.where(same, rep_scr[:, 128:256], 0.0).astype(BF16),
                    ],
                    axis=1,
                )
                moved = jnp.dot(left, grolled[q], preferred_element_type=F32).astype(BF16)
                weighed = jnp.where(shift < SHIFTS - 0.5, wsel_scr[...], 0.0).astype(BF16)
                both = jnp.concatenate([moved, weighed], axis=1)
                rhs[pl.ds(pl.multiple_of(q * 128, 128), 128), :] = both[0:128]
                rhs[pl.ds(pl.multiple_of(4096 + t * 128 + h * 64, 64), 64), :] = both[128:192]
        return 0

    lax.fori_loop(0, 4, patches, 0)

    diagonal = sublanes((128, 128)) == lanes((128, 128))

    def deposit(d, _):
        block = (x + d) % XN
        picked = ohs[pl.ds(pl.multiple_of(block * 128, 128), 128), :]
        total = jnp.dot(picked, rhs[...], preferred_element_type=F32)
        halves = total[:, 128:256]
        weighed = jnp.where(diagonal, halves + pltpu.roll(halves, 64, 1), 0.0)
        slot = d % XN
        xs[slot, 0:128, :] = total[:, 0:128]
        xs[slot, 128:136, :] = jnp.broadcast_to(jnp.sum(weighed, axis=0, keepdims=True), (8, 128))
        return 0

    x_copies = [
        pltpu.make_async_remote_copy(
            xs.at[d], xr.at[d - 1], x_send.at[d - 1], x_recv.at[d - 1],
            device_id=place((x + d) % XN, y, z, core),
        )
        for d in range(1, XN)
    ]
    for d in (2, 1, 3, 4):
        deposit(d, 0)
        if d < XN:
            x_copies[d - 1].start()
    for copy in x_copies:
        copy.wait_recv()
    brick = xs[0] + xr[0] + xr[1] + xr[2]

    first = y * swap + z * core
    second = z * swap + y * core
    for k in range(8):
        asd[k, 0:16, :] = brick[k * 16 : (k + 1) * 16]
        asd[k, 16:24, :] = brick[128:136]
    a_copies = [
        pltpu.make_async_remote_copy(
            asd.at[(first + d) % 8], ar.at[d - 1], a_send.at[d - 1], a_recv.at[d - 1],
            device_id=place(x, (y + swap * d) % YN, (z + core * d) % ZN, core),
        )
        for d in range(1, 8)
    ]
    for copy in a_copies:
        copy.start()
    for copy in a_copies:
        copy.wait_recv()
    lines = asd[first]
    for d in range(7):
        lines = lines + ar[d]

    sub8 = sublanes((8, 128))
    for k in range(8):
        tile = lines[8 * (k // 4) : 8 * (k // 4) + 8]
        turned = pltpu.roll(tile, 8 - 2 * (k % 4), 0) if k % 4 else tile
        bsd[k] = jnp.where(sub8 < 2, turned, lines[16:24])
    b_copies = [
        pltpu.make_async_remote_copy(
            bsd.at[(second + d) % 8], br.at[d - 1], b_send.at[d - 1], b_recv.at[d - 1],
            device_id=place(x, (y + core * d) % YN, (z + swap * d) % ZN, core),
        )
        for d in range(1, 8)
    ]
    for copy in b_copies:
        copy.start()
    for copy in b_copies:
        copy.wait_recv()
    last = bsd[second]
    for d in range(7):
        last = last + br[d]
    mine = lanes((2, 128)) == sublanes((2, 128)) + (first * 16 + second * 2)
    weight = jnp.sum(jnp.where(mine, last[2:4], 0.0), axis=1, keepdims=True)
    merged_out[...] = (last[0:2] + PRIOR * old_v[...]) / (weight + PRIOR)

    swap_frames.wait_send()
    for copy in (*p_copies, *s_copies, *x_copies, *a_copies, *b_copies):
        copy.wait_send()


def shards(photon_counts, slices, owner_ids, tile_ids, patch_count, old_model):
    dma = pltpu.SemaphoreType.DMA
    return pl.pallas_call(
        kernel,
        out_shape=(jax.ShapeDtypeStruct((16, 192), BF16), jax.ShapeDtypeStruct((2, 128), F32)),
        in_specs=[pl.BlockSpec(memory_space=pl.ANY)] * 6,
        out_specs=(pl.BlockSpec(memory_space=pltpu.VMEM), pl.BlockSpec(memory_space=pltpu.VMEM)),
        scratch_shapes=[
            pltpu.VMEM((16, 4096), jnp.int32),
            pltpu.VMEM((16, 4096), jnp.int32),
            pltpu.VMEM((192, 4096), BF16),
            pltpu.VMEM((192, 32), jnp.int32),
            pltpu.VMEM((192, 32), jnp.int32),
            pltpu.VMEM((1, 192), jnp.int32),
            pltpu.VMEM((2, 128), F32),
            pltpu.VMEM((256, 128), jnp.int32),
            pltpu.VMEM((16, 256), F32),
            pltpu.VMEM((192, 128), F32),
            pltpu.VMEM((192, 256), F32),
            pltpu.VMEM((192, 128), F32),
            pltpu.VMEM((32, 256, 128), BF16),
            pltpu.VMEM((48, 128), jnp.int32),
            pltpu.VMEM((ROWS, KTOT), BF16),
            pltpu.VMEM((KTOT, 256), BF16),
            pltpu.VMEM((24, 128), F32),
            pltpu.VMEM((3, 24, 128), F32),
            pltpu.VMEM((32, 128), F32),
            pltpu.VMEM((6, 8, 128), F32),
            pltpu.VMEM((32, 128), F32),
            pltpu.VMEM((4, 136, 128), F32),
            pltpu.VMEM((3, 136, 128), F32),
            pltpu.VMEM((8, 24, 128), F32),
            pltpu.VMEM((7, 24, 128), F32),
            pltpu.VMEM((8, 8, 128), F32),
            pltpu.VMEM((7, 8, 128), F32),
            dma((9,)),
            dma((1,)), dma((1,)),
            dma((3,)), dma((3,)),
            dma((7,)), dma((7,)),
            dma((3,)), dma((3,)),
            dma((7,)), dma((7,)),
            dma((7,)), dma((7,)),
        ],
        compiler_params=pltpu.CompilerParams(
            collective_id=0, has_side_effects=True, vmem_limit_bytes=40 * 1024 * 1024
        ),
        cost_estimate=pl.CostEstimate(flops=2 * 10**9, bytes_accessed=2 * 10**6, transcendentals=10**6),
        name="em_step",
    )(photon_counts, slices, owner_ids, tile_ids, patch_count.reshape(1, -1), old_model)


def solution(mesh):
    placed = (
        P("frame", "pix"),
        P("orient", "pix"),
        P("orient", "pix"),
        P("orient", "pix"),
        P("orient"),
        P(("frame", "orient", "pix"), None),
    )
    return jax.shard_map(
        shards,
        mesh=mesh,
        in_specs=placed,
        out_specs=(P("frame", "orient"), P(("frame", "orient", "pix"), None)),
        check_vma=False,
    )
```

time: 374 us -> 50.3 us (0.13)
  waiting for transfers between devices: 175 us -> 0 us
  blocking collectives: 105 us -> 0 us
  Pallas kernels: 0 us -> 42.3 us
  matrix products: 31.7 us -> 0 us
  other arithmetic: 21.5 us -> 0 us
  between operations: 14.2 us -> 0.65 us
  starting transfers between devices: 11.7 us -> 0 us
  local copies, waits for them, and re-layouts: 13.7 us -> 6.59 us
    unnamed x2 -> x0, waiting for transfers between devices: 165 us -> none
    unnamed x1 -> x0, blocking collectives: 105 us -> none
    pallas_call x0 -> x1, Pallas kernels: none -> 42.3 us  [shards(): pl.pallas_call(kernel, out_shape=(jax.ShapeDtypeStruct((16, 192), BF16),...]
    dot_general x10 -> x0, matrix products: 31.7 us -> none  [the longest x4 16.9 us: one_brick(): jnp.dot(onehot, flat_values, precision=lax.Precision.HIGHEST, preferred_e...]
    mul x5 -> x0, other arithmetic: 15.4 us -> none  [the longest x1 14.9 us: deposit(): flat_values = (moved * live_mask[:, :, None]).reshape(-1, 128)]
    all_to_all x2 -> x0, starting transfers between devices: 11.7 us -> none  [sent_to_all(): lax.all_to_all(jnp.broadcast_to(shard[None], (devices, *shard.shape)), ax...]
    all_to_all x2 -> x0, waiting for transfers between devices: 9.87 us -> none  [sent_to_all(): lax.all_to_all(jnp.broadcast_to(shard[None], (devices, *shard.shape)), ax...]
    slice x14 -> x0, local copies, waits for them, and re-layouts: 6.25 us -> none  [the longest x7 6.14 us: deposit(): rolled = jnp.roll(values, 17 * shift, axis=2)]
  transfers between devices with their start and end apart: 3 -> 0, of which waited for: 3 -> 0; matrix products, arithmetic and copies ran while one was open for 0% -> 0% of each run, Pallas kernels for 0% -> 0%
where the time goes in v1:
time: 50.3 us; the launch traced here: 49.6 us
  Pallas kernels  42.3 us (84%)
  local copies, waits for them, and re-layouts  6.59 us (13%)
  between operations  0.65 us (1%)
    pallas_call x1, Pallas kernels, shards(): pl.pallas_call(kernel, out_shape=(jax.ShapeDtypeStruct((16, 192), BF16),...  42.3 us
    unnamed x12, local copies, waits for them, and re-layouts  6.59 us

profile of v1, /device:TPU:1, one launch (start us, length us, event | category | flops | bytes accessed | tf_op | source)
XLA Modules:
  0.0 49.6 jit_solution(11197646059015431174)
XLA Ops:
  0.6 0.9 %copy.8.owner_in = s32[192,32]{1,0:T(8,128)S(1)} copy(s32[192,32]{0,1:T(8,128)} %param.8) | data formatting | bytes 49152 | tf_op args[2]
  1.5 0.9 %copy.9.tile_in = s32[192,32]{1,0:T(8,128)S(1)} copy(s32[192,32]{0,1:T(8,128)} %param.9) | data formatting | bytes 49152 | tf_op args[3]
  2.3 0.0 copy-start
  2.4 1.4 %copy-done = bf16[192,4096]{1,0:T(8,128)(2,1)S(1)} copy-done((bf16[192,4096]{1,0:T(8,128)(2,1)S(1)}, bf16[192,4096]{1,0:T(8,128)(2,1)}, u32[]{:S(2)}) %copy-start) | copy-done | bytes 1572888
  3.8 0.0 copy-start.1
  3.8 0.9 %copy-done.1 = s32[16,4096]{1,0:T(8,128)S(1)} copy-done((s32[16,4096]{1,0:T(8,128)S(1)}, s32[16,4096]{1,0:T(8,128)}, u32[]{:S(2)}) %copy-start.1) | copy-done | bytes 262168
  4.7 0.0 copy-start.2
  4.7 0.7 %copy-done.2 = s32[192]{0:T(256)S(1)} copy-done((s32[192]{0:T(256)S(1)}, s32[192]{0:T(256)}, u32[]{:S(2)}) %copy-start.2) | copy-done | bytes 792
  5.4 0.0 copy-start.3
  5.4 0.7 %copy-done.3 = f32[2,128]{1,0:T(2,128)S(1)} copy-done((f32[2,128]{1,0:T(2,128)S(1)}, f32[2,128]{1,0:T(2,128)}, u32[]{:S(2)}) %copy-start.3) | copy-done | bytes 1048
  6.1 42.3 %em_step.1 = (bf16[16,192]{1,0:T(8,128)(2,1)S(1)}, f32[2,128]{1,0:T(2,128)S(1)}) custom-call(s32[16,4096]{1,0:T(8,128)S(1)} %copy-done.1, bf16[192,4096]{1,0:T(8,128)(2,1)S(1)} %copy-done, s32[192,32]{1,0:T(8,128)S(1)} %copy.8.owner_in, s32[192,32]{1,0:T(8,128)S(1)} %copy.9.tile_in, s32[1,192]{1,0:T(1,128)S(1)} %bitcast.1, f32[2,128]{1,0:T(2,128)S(1)} %copy-done.3), custom_call_target="tpu_custom_call" | custom-call | flops 2000000000 | bytes 2000000 | tf_op jit(solution)/shard_map/em_step/pallas_call | solution.py:346
  48.4 0.6 %copy.12 = bf16[16,192]{1,0:T(8,128)(2,1)} copy(bf16[16,192]{1,0:T(8,128)(2,1)S(1)} %get-tuple-element.4) | data formatting | bytes 12288
  49.0 0.6 %copy.13 = f32[2,128]{1,0:T(2,128)} copy(f32[2,128]{1,0:T(2,128)S(1)} %get-tuple-element.5) | data formatting | bytes 2048
Async XLA Ops:
  2.3 1.4 %copy-start = (bf16[192,4096]{1,0:T(8,128)(2,1)S(1)}, bf16[192,4096]{1,0:T(8,128)(2,1)}, u32[]{:S(2)}) copy-start(bf16[192,4096]{1,0:T(8,128)(2,1)} %slices_in.1) | copy-start | bytes 4718596
  3.8 0.9 %copy-start.1 = (s32[16,4096]{1,0:T(8,128)S(1)}, s32[16,4096]{1,0:T(8,128)}, u32[]{:S(2)}) copy-start(s32[16,4096]{1,0:T(8,128)} %counts_in.1) | copy-start | bytes 786436
  4.7 0.7 %copy-start.2 = (s32[192]{0:T(256)S(1)}, s32[192]{0:T(256)}, u32[]{:S(2)}) copy-start(s32[192]{0:T(256)} %param.10) | copy-start | bytes 2308
  5.4 0.7 %copy-start.3 = (f32[2,128]{1,0:T(2,128)S(1)}, f32[2,128]{1,0:T(2,128)}, u32[]{:S(2)}) copy-start(f32[2,128]{1,0:T(2,128)} %old_in.1) | copy-start | bytes 3076

commit v2 on v1

--- a/solution.py
+++ b/solution.py
@@ -9,7 +9,8 @@
 from jax.sharding import PartitionSpec as P
 
 XN, YN, ZN = 4, 8, 8
-PEERS_X = XN - 1
+FAR8 = (4, 3, 5, 2, 6, 1, 7)
+FAR4 = (2, 1, 3, 0)
 PIXELS = 16384
 SHIFTS = 8
 PRIOR = 512 * 128 / (4.0 * 1024)
@@ -34,8 +35,8 @@
     cnt, pcnt, sl, own_v, til_v, pc_v, old_v,
     idpad, fit_scr, shm_scr, rep_scr, wsel_scr, grolled, rowk, ohs, rhs,
     psend, precv, ssend, srecv, ppart,
-    xs, xr, asd, ar, bsd, br,
-    loc_sem, fr_send, fr_recv, p_send, p_recv, s_send, s_recv, x_send, x_recv, a_send, a_recv, b_send, b_recv,
+    xs, xr, bsd, br,
+    loc_sem, fr_send, fr_recv, p_send, p_recv, s_send, s_recv, x_send, x_recv, b_send, b_recv,
 ):
     fi = lax.axis_index("frame")
     x = lax.axis_index("orient")
@@ -48,6 +49,9 @@
 
     def place(xx, yy, zz, cc):
         return {"frame": zz * 4 + (yy % 2) * 2 + cc, "orient": xx, "pix": yy // 2}
+
+    def along_first(dx, df):
+        return place((x + dx) % XN, (y + swap * df) % YN, (z + core * df) % ZN, core)
 
     locals_ = [
         pltpu.make_async_copy(counts_in, cnt, loc_sem.at[0]),
@@ -66,14 +70,15 @@
         copy.start()
 
     barrier = pltpu.get_barrier_semaphore()
+    for d in FAR8:
+        pl.semaphore_signal(barrier, inc=1, device_id=place(x, (y + core * d) % YN, (z + swap * d) % ZN, core))
+    for df in (*FAR8, 0):
+        for dx in FAR4:
+            if dx or df:
+                pl.semaphore_signal(barrier, inc=1, device_id=along_first(dx, df))
+    for d in FAR4[:3]:
+        pl.semaphore_signal(barrier, inc=1, device_id=place((x + d) % XN, y, z, swap))
     pl.semaphore_signal(barrier, inc=1, device_id=place(x, y, z, swap))
-    for d in range(1, XN):
-        for cc in (core, swap):
-            pl.semaphore_signal(barrier, inc=1, device_id=place((x + d) % XN, y, z, cc))
-    for d in range(1, YN):
-        pl.semaphore_signal(barrier, inc=1, device_id=place(x, (y + d) % YN, z, core))
-    for d in range(1, ZN):
-        pl.semaphore_signal(barrier, inc=1, device_id=place(x, y, (z + d) % ZN, core))
 
     locals_[0].wait()
     fit = jnp.zeros((16, 192), F32)
@@ -94,14 +99,14 @@
     psend[0:16, :] = fit_scr[:, 0:128]
     psend[16:24, :] = jnp.where(lane8 < 64, fit_scr[0:8, 128:256], pltpu.roll(fit_scr[8:16, 128:256], 64, 1))
 
-    pl.semaphore_wait(barrier, 1 + 2 * PEERS_X + (YN - 1) + (ZN - 1))
+    pl.semaphore_wait(barrier, 7 + 31 + 3 + 1)
 
     p_copies = [
         pltpu.make_async_remote_copy(
             psend, precv.at[d - 1], p_send.at[d - 1], p_recv.at[d - 1],
             device_id=place(x, (y + 2 * d) % YN, z, core),
         )
-        for d in range(1, 4)
+        for d in (2, 1, 3)
     ]
     for copy in p_copies:
         copy.start()
@@ -116,22 +121,23 @@
     rid = own_v[...] * 256 + (tid >> 3)
     ry = ((rid >> 1) & 3) * 2 + ((rid >> 6) & 1)
     rz = rid >> 7
-    spot = ((rid >> 3) & 3) * 128 + (ry * swap + rz * core) * 16 + (rz * swap + ry * core) * 2 + (rid & 1)
+    dx = (((rid >> 3) & 3) - x) & 3
+    block = jnp.where(dx == 2, 0, jnp.where(dx == 0, 3, (dx + 1) >> 1))
+    first_step = (ry * swap + rz * core - (y * swap + z * core)) & 7
+    second_step = (rz * swap + ry * core - (z * swap + y * core)) & 7
+    spot = block * 128 + first_step * 16 + second_step * 2 + (rid & 1)
     spot = jnp.where(((rid >> 5) & 1) == core, spot, -1)
-    idpad[...] = jnp.zeros((256, 128), jnp.int32)
-    idpad[0:192, 0:32] = spot
-    turned = jnp.transpose(idpad[...])
-    rowk[0:32, :] = turned[0:32, 0:128]
+    idpad[...] = jnp.zeros((32, 256), jnp.int32)
+    idpad[:, 0:192] = spot
+    rowk[0:32, :] = idpad[:, 0:128]
     rowk[32:48, :] = jnp.where(
-        lanes((16, 128)) < 64, turned[0:16, 128:256], pltpu.roll(turned[16:32, 128:256], 64, 1)
-    )
+        lanes((16, 128)) < 64, idpad[0:16, 128:256], pltpu.roll(idpad[16:32, 128:256], 64, 1)
+    )
+    live = sublanes((32, 192)) + y_hi * 32 < jnp.broadcast_to(pc_v[...], (32, 192))
+    shift_rows = jnp.where(live, tid & 7, SHIFTS).astype(F32)
+    shift_rows = jnp.concatenate([shift_rows, jnp.full((96, 192), float(SHIFTS), F32)], axis=0)
     eye = (sublanes((192, 192)) == lanes((192, 192))).astype(F32).astype(BF16)
-    pc_col = lax.dot_general(
-        eye, jnp.broadcast_to(pc_v[...].astype(F32), (128, 192)).astype(BF16), NT, preferred_element_type=F32
-    )
-    shm_scr[...] = jnp.full((192, 128), float(SHIFTS), F32)
-    live = (lanes((192, 32)) + y_hi * 32).astype(F32) < pc_col[:, 0:32]
-    shm_scr[:, 0:32] = jnp.where(live, (tid & 7).astype(F32), float(SHIFTS))
+    shm_scr[...] = lax.dot_general(eye, shift_rows.astype(BF16), NT, preferred_element_type=F32)
 
     def roll_frames(source, half):
         def body(q, _):
@@ -180,7 +186,7 @@
     ssend[8:24, :] = exp_a
     ssend[24:32, :] = jnp.where(lane8 < 64, exp_b[0:8], pltpu.roll(exp_b[8:16], 64, 1))
     s_copies = []
-    for d in range(1, XN):
+    for d in FAR4[:3]:
         for rel, cc in enumerate((core, swap)):
             slot = (d - 1) * 2 + rel
             s_copies.append(
@@ -232,32 +238,30 @@
     )
     eye = (sublanes((192, 256)) == lanes((192, 256))).astype(F32).astype(BF16)
     rep = lax.dot_general(eye, stack, NT, preferred_element_type=F32)
-    rep_scr[...] = rep
+    rep_scr[...] = rep.astype(BF16)
     lane_shift = (lanes((192, 256)) % 128) // 16
     weights = jnp.dot(
         jnp.where(lane_shift == 0, rep, 0.0).astype(BF16), jnp.ones((256, 128), BF16), preferred_element_type=F32
     )
     upper = weights.astype(BF16).astype(F32)
-    wsel_scr[...] = jnp.where(lanes((192, 128)) < 64, upper, weights - upper)
+    wsel_scr[...] = jnp.where(lanes((192, 128)) < 64, upper, weights - upper).astype(BF16)
 
     def patches(t4, _):
         columns = pltpu.roll(shm_scr[...], 128 - 4 * t4, 1)
+        lane = ((lanes((192, 128)) % 128) // 16).astype(F32).astype(BF16)
+        nil = jnp.zeros((192, 128), BF16)
+        limit = jnp.full((192, 128), SHIFTS, BF16)
         for u in range(4):
             t = t4 * 4 + u
             for h in range(2):
                 q = t + 16 * h
-                shift = jnp.broadcast_to(columns[:, u + 16 * h : u + 16 * h + 1], (192, 128))
-                lane = ((lanes((192, 128)) % 128) // 16).astype(F32)
+                shift = jnp.broadcast_to(columns[:, u + 16 * h : u + 16 * h + 1], (192, 128)).astype(BF16)
                 same = shift == lane
                 left = jnp.concatenate(
-                    [
-                        jnp.where(same, rep_scr[:, 0:128], 0.0).astype(BF16),
-                        jnp.where(same, rep_scr[:, 128:256], 0.0).astype(BF16),
-                    ],
-                    axis=1,
+                    [jnp.where(same, rep_scr[:, 0:128], nil), jnp.where(same, rep_scr[:, 128:256], nil)], axis=1
                 )
                 moved = jnp.dot(left, grolled[q], preferred_element_type=F32).astype(BF16)
-                weighed = jnp.where(shift < SHIFTS - 0.5, wsel_scr[...], 0.0).astype(BF16)
+                weighed = jnp.where(shift < limit, wsel_scr[...], nil)
                 both = jnp.concatenate([moved, weighed], axis=1)
                 rhs[pl.ds(pl.multiple_of(q * 128, 128), 128), :] = both[0:128]
                 rhs[pl.ds(pl.multiple_of(4096 + t * 128 + h * 64, 64), 64), :] = both[128:192]
@@ -266,78 +270,56 @@
     lax.fori_loop(0, 4, patches, 0)
 
     diagonal = sublanes((128, 128)) == lanes((128, 128))
-
-    def deposit(d, _):
-        block = (x + d) % XN
-        picked = ohs[pl.ds(pl.multiple_of(block * 128, 128), 128), :]
-        total = jnp.dot(picked, rhs[...], preferred_element_type=F32)
+    x_copies = []
+    for block, dx in enumerate(FAR4):
+        total = jnp.dot(ohs[block * 128 : (block + 1) * 128, :], rhs[...], preferred_element_type=F32)
         halves = total[:, 128:256]
         weighed = jnp.where(diagonal, halves + pltpu.roll(halves, 64, 1), 0.0)
-        slot = d % XN
-        xs[slot, 0:128, :] = total[:, 0:128]
-        xs[slot, 128:136, :] = jnp.broadcast_to(jnp.sum(weighed, axis=0, keepdims=True), (8, 128))
-        return 0
-
-    x_copies = [
-        pltpu.make_async_remote_copy(
-            xs.at[d], xr.at[d - 1], x_send.at[d - 1], x_recv.at[d - 1],
-            device_id=place((x + d) % XN, y, z, core),
-        )
-        for d in range(1, XN)
-    ]
-    for d in (2, 1, 3, 4):
-        deposit(d, 0)
-        if d < XN:
-            x_copies[d - 1].start()
-    for copy in x_copies:
+        line = jnp.broadcast_to(jnp.sum(weighed, axis=0, keepdims=True), (8, 128))
+        for df in range(8):
+            xs[block * 8 + df, 0:16, :] = total[df * 16 : (df + 1) * 16, 0:128]
+            xs[block * 8 + df, 16:24, :] = pltpu.roll(line, 128 - 16 * df, 1) if df else line
+        for df in (*FAR8, 0):
+            if dx == 0 and df == 0:
+                continue
+            at = block * 8 + df
+            slot = at if dx else at - 1
+            copy = pltpu.make_async_remote_copy(
+                xs.at[at, 0:17], xr.at[slot, 0:17], x_send.at[slot], x_recv.at[slot], device_id=along_first(dx, df)
+            )
+            copy.start()
+            x_copies.append((slot, copy))
+    brick = xs[24]
+    for slot, copy in x_copies:
         copy.wait_recv()
-    brick = xs[0] + xr[0] + xr[1] + xr[2]
-
-    first = y * swap + z * core
-    second = z * swap + y * core
-    for k in range(8):
-        asd[k, 0:16, :] = brick[k * 16 : (k + 1) * 16]
-        asd[k, 16:24, :] = brick[128:136]
-    a_copies = [
-        pltpu.make_async_remote_copy(
-            asd.at[(first + d) % 8], ar.at[d - 1], a_send.at[d - 1], a_recv.at[d - 1],
-            device_id=place(x, (y + swap * d) % YN, (z + core * d) % ZN, core),
-        )
-        for d in range(1, 8)
-    ]
-    for copy in a_copies:
-        copy.start()
-    for copy in a_copies:
-        copy.wait_recv()
-    lines = asd[first]
-    for d in range(7):
-        lines = lines + ar[d]
+        brick = brick + xr[slot]
+    x_copies = [copy for _, copy in x_copies]
 
     sub8 = sublanes((8, 128))
     for k in range(8):
-        tile = lines[8 * (k // 4) : 8 * (k // 4) + 8]
-        turned = pltpu.roll(tile, 8 - 2 * (k % 4), 0) if k % 4 else tile
-        bsd[k] = jnp.where(sub8 < 2, turned, lines[16:24])
+        tile = brick[8 * (k // 4) : 8 * (k // 4) + 8]
+        tile = pltpu.roll(tile, 8 - 2 * (k % 4), 0) if k % 4 else tile
+        line = jnp.broadcast_to(brick[16:17], (8, 128))
+        line = pltpu.roll(line, 128 - 2 * k, 1) if k else line
+        bsd[k] = jnp.where(sub8 < 2, tile, line)
     b_copies = [
         pltpu.make_async_remote_copy(
-            bsd.at[(second + d) % 8], br.at[d - 1], b_send.at[d - 1], b_recv.at[d - 1],
+            bsd.at[d], br.at[d - 1], b_send.at[d - 1], b_recv.at[d - 1],
             device_id=place(x, (y + core * d) % YN, (z + swap * d) % ZN, core),
         )
-        for d in range(1, 8)
+        for d in FAR8
     ]
     for copy in b_copies:
         copy.start()
-    for copy in b_copies:
+    last = bsd[0]
+    for d, copy in zip(FAR8, b_copies):
         copy.wait_recv()
-    last = bsd[second]
-    for d in range(7):
-        last = last + br[d]
-    mine = lanes((2, 128)) == sublanes((2, 128)) + (first * 16 + second * 2)
-    weight = jnp.sum(jnp.where(mine, last[2:4], 0.0), axis=1, keepdims=True)
+        last = last + br[d - 1]
+    weight = jnp.sum(jnp.where(lanes((2, 128)) == sublanes((2, 128)), last[2:4], 0.0), axis=1, keepdims=True)
     merged_out[...] = (last[0:2] + PRIOR * old_v[...]) / (weight + PRIOR)
 
     swap_frames.wait_send()
-    for copy in (*p_copies, *s_copies, *x_copies, *a_copies, *b_copies):
+    for copy in (*p_copies, *s_copies, *x_copies, *b_copies):
         copy.wait_send()
 
 
@@ -352,15 +334,15 @@
             pltpu.VMEM((16, 4096), jnp.int32),
             pltpu.VMEM((16, 4096), jnp.int32),
             pltpu.VMEM((192, 4096), BF16),
-            pltpu.VMEM((192, 32), jnp.int32),
-            pltpu.VMEM((192, 32), jnp.int32),
+            pltpu.VMEM((32, 192), jnp.int32),
+            pltpu.VMEM((32, 192), jnp.int32),
             pltpu.VMEM((1, 192), jnp.int32),
             pltpu.VMEM((2, 128), F32),
-            pltpu.VMEM((256, 128), jnp.int32),
+            pltpu.VMEM((32, 256), jnp.int32),
             pltpu.VMEM((16, 256), F32),
             pltpu.VMEM((192, 128), F32),
-            pltpu.VMEM((192, 256), F32),
-            pltpu.VMEM((192, 128), F32),
+            pltpu.VMEM((192, 256), BF16),
+            pltpu.VMEM((192, 128), BF16),
             pltpu.VMEM((32, 256, 128), BF16),
             pltpu.VMEM((48, 128), jnp.int32),
             pltpu.VMEM((ROWS, KTOT), BF16),
@@ -370,26 +352,23 @@
             pltpu.VMEM((32, 128), F32),
             pltpu.VMEM((6, 8, 128), F32),
             pltpu.VMEM((32, 128), F32),
-            pltpu.VMEM((4, 136, 128), F32),
-            pltpu.VMEM((3, 136, 128), F32),
-            pltpu.VMEM((8, 24, 128), F32),
-            pltpu.VMEM((7, 24, 128), F32),
+            pltpu.VMEM((32, 24, 128), F32),
+            pltpu.VMEM((31, 24, 128), F32),
             pltpu.VMEM((8, 8, 128), F32),
             pltpu.VMEM((7, 8, 128), F32),
             dma((9,)),
             dma((1,)), dma((1,)),
             dma((3,)), dma((3,)),
             dma((7,)), dma((7,)),
-            dma((3,)), dma((3,)),
-            dma((7,)), dma((7,)),
+            dma((31,)), dma((31,)),
             dma((7,)), dma((7,)),
         ],
         compiler_params=pltpu.CompilerParams(
-            collective_id=0, has_side_effects=True, vmem_limit_bytes=40 * 1024 * 1024
+            collective_id=0, has_side_effects=True, vmem_limit_bytes=60 * 1024 * 1024
         ),
         cost_estimate=pl.CostEstimate(flops=2 * 10**9, bytes_accessed=2 * 10**6, transcendentals=10**6),
         name="em_step",
-    )(photon_counts, slices, owner_ids, tile_ids, patch_count.reshape(1, -1), old_model)
+    )(photon_counts, slices, owner_ids.T, tile_ids.T, patch_count.reshape(1, -1), old_model)
 
 
 def solution(mesh):

time: 50.3 us -> 44.2 us (0.88)
  local copies, waits for them, and re-layouts: 6.59 us -> 2.51 us
  Pallas kernels: 42.3 us -> 40.8 us
    unnamed x12 -> x2, local copies, waits for them, and re-layouts: 6.59 us -> 2.51 us
    pallas_call x1, Pallas kernels: 42.3 us -> 40.8 us  [shards(): pl.pallas_call(kernel, out_shape=(jax.ShapeDtypeStruct((16, 192), BF16),...]
where the time goes in v2:
time: 44.2 us; the launch traced here: 44 us
  Pallas kernels  40.8 us (92%)
  local copies, waits for them, and re-layouts  2.51 us (6%)
  between operations  0.64 us (1%)
    pallas_call x1, Pallas kernels, shards(): pl.pallas_call(kernel, out_shape=(jax.ShapeDtypeStruct((16, 192), BF16),...  40.8 us
    unnamed x2, local copies, waits for them, and re-layouts  2.51 us

profile of v2, /device:TPU:1, one launch (start us, length us, event | category | flops | bytes accessed | tf_op | source)
XLA Modules:
  0.0 44.0 jit_solution(14857588892596775108)
XLA Ops:
  0.6 40.8 %em_step.1 = (bf16[16,192]{1,0:T(8,128)(2,1)}, f32[2,128]{1,0:T(2,128)}) custom-call(s32[16,4096]{1,0:T(8,128)} %counts_in.1, bf16[192,4096]{1,0:T(8,128)(2,1)} %slices_in.1, s32[32,192]{1,0:T(8,128)} %bitcast.3, s32[32,192]{1,0:T(8,128)} %bitcast.4, s32[1,192]{1,0:T(1,128)} %bitcast.5, f32[2,128]{1,0:T(2,128)} %old_in.1), custom_call_target="tpu_custom_call" | custom-call | flops 2000000000 | bytes 2000000 | tf_op jit(solution)/shard_map/em_step/pallas_call | solution.py:328
  41.4 1.3 %copy.10 = bf16[16,192]{1,0:T(8,128)(2,1)} copy(bf16[16,192]{1,0:T(8,128)(2,1)} %get-tuple-element.4) | data formatting | bytes 12288
  42.7 1.2 %copy.11 = f32[2,128]{1,0:T(2,128)} copy(f32[2,128]{1,0:T(2,128)} %get-tuple-element.5) | data formatting | bytes 2048

commit v3 on v2

--- a/solution.py
+++ b/solution.py
@@ -11,6 +11,9 @@
 XN, YN, ZN = 4, 8, 8
 FAR8 = (4, 3, 5, 2, 6, 1, 7)
 FAR4 = (2, 1, 3, 0)
+PLACES = sorted(
+    ((dx, df) for df in range(8) for dx in range(4)), key=lambda p: -min(p[0], 4 - p[0]) - min(p[1], 8 - p[1])
+)
 PIXELS = 16384
 SHIFTS = 8
 PRIOR = 512 * 128 / (4.0 * 1024)
@@ -33,7 +36,7 @@
     counts_in, slices_in, owner_in, tile_in, count_in, old_in,
     prob_out, merged_out,
     cnt, pcnt, sl, own_v, til_v, pc_v, old_v,
-    idpad, fit_scr, shm_scr, rep_scr, wsel_scr, grolled, rowk, ohs, rhs,
+    idpad, fit_scr, shm_scr, rep_scr, wsel_scr, col_scr, lhs, grolled, rowk, ohs, rhs,
     psend, precv, ssend, srecv, ppart,
     xs, xr, bsd, br,
     loc_sem, fr_send, fr_recv, p_send, p_recv, s_send, s_recv, x_send, x_recv, b_send, b_recv,
@@ -72,10 +75,8 @@
     barrier = pltpu.get_barrier_semaphore()
     for d in FAR8:
         pl.semaphore_signal(barrier, inc=1, device_id=place(x, (y + core * d) % YN, (z + swap * d) % ZN, core))
-    for df in (*FAR8, 0):
-        for dx in FAR4:
-            if dx or df:
-                pl.semaphore_signal(barrier, inc=1, device_id=along_first(dx, df))
+    for dx, df in PLACES[:31]:
+        pl.semaphore_signal(barrier, inc=1, device_id=along_first(dx, df))
     for d in FAR4[:3]:
         pl.semaphore_signal(barrier, inc=1, device_id=place((x + d) % XN, y, z, swap))
     pl.semaphore_signal(barrier, inc=1, device_id=place(x, y, z, swap))
@@ -122,10 +123,13 @@
     ry = ((rid >> 1) & 3) * 2 + ((rid >> 6) & 1)
     rz = rid >> 7
     dx = (((rid >> 3) & 3) - x) & 3
-    block = jnp.where(dx == 2, 0, jnp.where(dx == 0, 3, (dx + 1) >> 1))
     first_step = (ry * swap + rz * core - (y * swap + z * core)) & 7
     second_step = (rz * swap + ry * core - (z * swap + y * core)) & 7
-    spot = block * 128 + first_step * 16 + second_step * 2 + (rid & 1)
+    where_to = dx * 8 + first_step
+    spot = jnp.full((32, 192), 31 * 16, jnp.int32)
+    for at, (dx, df) in enumerate(PLACES[:31]):
+        spot = jnp.where(where_to == dx * 8 + df, at * 16, spot)
+    spot = spot + second_step * 2 + (rid & 1)
     spot = jnp.where(((rid >> 5) & 1) == core, spot, -1)
     idpad[...] = jnp.zeros((32, 256), jnp.int32)
     idpad[:, 0:192] = spot
@@ -162,7 +166,9 @@
         lax.fori_loop(first, last, body, 0, unroll=2)
 
     roll_frames(cnt, 0)
-    onehot(0, 16)
+    onehot(0, 48)
+    swap_frames.wait_recv()
+    roll_frames(pcnt, 1)
 
     for copy in p_copies:
         copy.wait_recv()
@@ -203,14 +209,40 @@
     for copy in s_copies:
         copy.start()
 
-    swap_frames.wait_recv()
-    roll_frames(pcnt, 1)
-    onehot(16, 48)
-
-    for copy in s_copies:
+    s_copies[-1].wait_recv()
+
+    def spread(packed):
+        tail = packed[24:32, :]
+        tail = jnp.concatenate([tail, pltpu.roll(tail, 64, 1)], axis=0)
+        both = jnp.concatenate([packed[8:24, :], tail], axis=1).astype(BF16)
+        return [both] * SHIFTS
+
+    eye = (sublanes((192, 256)) == lanes((192, 256))).astype(F32).astype(BF16)
+    stack = jnp.concatenate(spread(ssend) + spread(ppart), axis=0)
+    rep_scr[...] = lax.dot_general(eye, stack, NT, preferred_element_type=F32).astype(BF16)
+
+    def selections(t4, _):
+        columns = pltpu.roll(shm_scr[...], 128 - 4 * t4, 1)
+        lane = ((lanes((192, 128)) % 128) // 16).astype(F32).astype(BF16)
+        nil = jnp.zeros((192, 128), BF16)
+        one = jnp.ones((192, 128), BF16)
+        limit = jnp.full((192, 128), SHIFTS, BF16)
+        for u in range(4):
+            for h in range(2):
+                q = t4 * 4 + u + 16 * h
+                shift = jnp.broadcast_to(columns[:, u + 16 * h : u + 16 * h + 1], (192, 128)).astype(BF16)
+                same = shift == lane
+                lhs[q, :, 0:128] = jnp.where(same, rep_scr[:, 0:128], nil)
+                lhs[q, :, 128:256] = jnp.where(same, rep_scr[:, 128:256], nil)
+                lhs[q, :, 256:384] = jnp.where(shift < limit, one, nil)
+        return 0
+
+    lax.fori_loop(0, 4, selections, 0)
+
+    for copy in s_copies[:-1]:
         copy.wait_recv()
 
-    def probabilities(packed, others):
+    def factors(packed, others):
         stats = packed[0:8, :]
         every = [stats, *others]
         most = functools.reduce(jnp.maximum, every)
@@ -219,50 +251,28 @@
         for other in others:
             whole = whole + other * pltpu.roll(jnp.exp(other - most), 32, 1)
         factor = scale / whole
-        low, high = factor[:, 32:33], factor[:, 96:97]
-        prob_a = jnp.concatenate([packed[8:16, :] * low, packed[16:24, :] * high], axis=0)
-        tail = packed[24:32, :]
-        prob_b = jnp.concatenate([tail * low, pltpu.roll(tail, 64, 1) * high], axis=0)
-        return prob_a.astype(BF16), prob_b.astype(BF16)
-
-    own_a, own_b = probabilities(ssend, [srecv[0], srecv[2], srecv[4]])
-    her_a, her_b = probabilities(ppart, [srecv[1], srecv[3], srecv[5]])
-    prob_out[:, 0:128] = own_a
-    prob_out[:, 128:192] = own_b[:, 0:64]
-
-    stack = jnp.concatenate(
-        [
-            jnp.concatenate([own_a, own_b], axis=1)] * SHIFTS + [
-            jnp.concatenate([her_a, her_b], axis=1)] * SHIFTS,
-        axis=0,
-    )
-    eye = (sublanes((192, 256)) == lanes((192, 256))).astype(F32).astype(BF16)
-    rep = lax.dot_general(eye, stack, NT, preferred_element_type=F32)
-    rep_scr[...] = rep.astype(BF16)
-    lane_shift = (lanes((192, 256)) % 128) // 16
-    weights = jnp.dot(
-        jnp.where(lane_shift == 0, rep, 0.0).astype(BF16), jnp.ones((256, 128), BF16), preferred_element_type=F32
-    )
+        return jnp.broadcast_to(factor[:, 32:33], (8, 128)), jnp.broadcast_to(factor[:, 96:97], (8, 128))
+
+    low, high = factors(ssend, [srecv[0], srecv[2], srecv[4]])
+    her_low, her_high = factors(ppart, [srecv[1], srecv[3], srecv[5]])
+    column = jnp.concatenate([low, high] * SHIFTS + [her_low, her_high] * SHIFTS, axis=0)
+    col_scr[...] = column
+    upper = column.astype(BF16).astype(F32)
+    parts = jnp.where(lanes((256, 128)) < 64, upper, column - upper).astype(BF16)
+    unshifted = jnp.where((lanes((192, 256)) % 128) // 16 == 0, rep_scr[...].astype(F32), 0.0).astype(BF16)
+    weights = jnp.dot(unshifted, parts, preferred_element_type=F32)
+    weights = weights + pltpu.roll(weights, 64, 1)
     upper = weights.astype(BF16).astype(F32)
     wsel_scr[...] = jnp.where(lanes((192, 128)) < 64, upper, weights - upper).astype(BF16)
 
     def patches(t4, _):
-        columns = pltpu.roll(shm_scr[...], 128 - 4 * t4, 1)
-        lane = ((lanes((192, 128)) % 128) // 16).astype(F32).astype(BF16)
-        nil = jnp.zeros((192, 128), BF16)
-        limit = jnp.full((192, 128), SHIFTS, BF16)
         for u in range(4):
             t = t4 * 4 + u
             for h in range(2):
                 q = t + 16 * h
-                shift = jnp.broadcast_to(columns[:, u + 16 * h : u + 16 * h + 1], (192, 128)).astype(BF16)
-                same = shift == lane
-                left = jnp.concatenate(
-                    [jnp.where(same, rep_scr[:, 0:128], nil), jnp.where(same, rep_scr[:, 128:256], nil)], axis=1
-                )
-                moved = jnp.dot(left, grolled[q], preferred_element_type=F32).astype(BF16)
-                weighed = jnp.where(shift < limit, wsel_scr[...], nil)
-                both = jnp.concatenate([moved, weighed], axis=1)
+                scaled = (grolled[q].astype(F32) * col_scr[...]).astype(BF16)
+                moved = jnp.dot(lhs[q, :, 0:256], scaled, preferred_element_type=F32).astype(BF16)
+                both = jnp.concatenate([moved, lhs[q, :, 256:384] * wsel_scr[...]], axis=1)
                 rhs[pl.ds(pl.multiple_of(q * 128, 128), 128), :] = both[0:128]
                 rhs[pl.ds(pl.multiple_of(4096 + t * 128 + h * 64, 64), 64), :] = both[128:192]
         return 0
@@ -271,29 +281,27 @@
 
     diagonal = sublanes((128, 128)) == lanes((128, 128))
     x_copies = []
-    for block, dx in enumerate(FAR4):
+    for block in range(4):
         total = jnp.dot(ohs[block * 128 : (block + 1) * 128, :], rhs[...], preferred_element_type=F32)
         halves = total[:, 128:256]
         weighed = jnp.where(diagonal, halves + pltpu.roll(halves, 64, 1), 0.0)
         line = jnp.broadcast_to(jnp.sum(weighed, axis=0, keepdims=True), (8, 128))
-        for df in range(8):
-            xs[block * 8 + df, 0:16, :] = total[df * 16 : (df + 1) * 16, 0:128]
-            xs[block * 8 + df, 16:24, :] = pltpu.roll(line, 128 - 16 * df, 1) if df else line
-        for df in (*FAR8, 0):
-            if dx == 0 and df == 0:
-                continue
-            at = block * 8 + df
-            slot = at if dx else at - 1
+        for k in range(8):
+            xs[block * 8 + k, 0:16, :] = total[k * 16 : (k + 1) * 16, 0:128]
+            xs[block * 8 + k, 16:24, :] = pltpu.roll(line, 128 - 16 * k, 1) if k else line
+        for at in range(block * 8, min(block * 8 + 8, 31)):
             copy = pltpu.make_async_remote_copy(
-                xs.at[at, 0:17], xr.at[slot, 0:17], x_send.at[slot], x_recv.at[slot], device_id=along_first(dx, df)
+                xs.at[at, 0:17], xr.at[at, 0:17], x_send.at[at], x_recv.at[at], device_id=along_first(*PLACES[at])
             )
             copy.start()
-            x_copies.append((slot, copy))
-    brick = xs[24]
-    for slot, copy in x_copies:
+            x_copies.append(copy)
+    tail = ssend[24:32, :]
+    prob_out[:, 0:128] = jnp.concatenate([ssend[8:16, :] * low, ssend[16:24, :] * high], axis=0).astype(BF16)
+    prob_out[:, 128:192] = jnp.concatenate([tail * low, pltpu.roll(tail, 64, 1) * high], axis=0)[:, 0:64].astype(BF16)
+    brick = xs[31]
+    for at, copy in enumerate(x_copies):
         copy.wait_recv()
-        brick = brick + xr[slot]
-    x_copies = [copy for _, copy in x_copies]
+        brick = brick + xr[at]
 
     sub8 = sublanes((8, 128))
     for k in range(8):
@@ -323,9 +331,17 @@
         copy.wait_send()
 
 
+def hand_on(prob_in, merged_in, prob_out, merged_out, sem):
+    copies = [pltpu.make_async_copy(prob_in, prob_out, sem.at[0]), pltpu.make_async_copy(merged_in, merged_out, sem.at[1])]
+    for copy in copies:
+        copy.start()
+    for copy in copies:
+        copy.wait()
+
+
 def shards(photon_counts, slices, owner_ids, tile_ids, patch_count, old_model):
     dma = pltpu.SemaphoreType.DMA
-    return pl.pallas_call(
+    prob, merged = pl.pallas_call(
         kernel,
         out_shape=(jax.ShapeDtypeStruct((16, 192), BF16), jax.ShapeDtypeStruct((2, 128), F32)),
         in_specs=[pl.BlockSpec(memory_space=pl.ANY)] * 6,
@@ -343,6 +359,8 @@
             pltpu.VMEM((192, 128), F32),
             pltpu.VMEM((192, 256), BF16),
             pltpu.VMEM((192, 128), BF16),
+            pltpu.VMEM((256, 128), F32),
+            pltpu.VMEM((32, 192, 384), BF16),
             pltpu.VMEM((32, 256, 128), BF16),
             pltpu.VMEM((48, 128), jnp.int32),
             pltpu.VMEM((ROWS, KTOT), BF16),
@@ -369,6 +387,16 @@
         cost_estimate=pl.CostEstimate(flops=2 * 10**9, bytes_accessed=2 * 10**6, transcendentals=10**6),
         name="em_step",
     )(photon_counts, slices, owner_ids.T, tile_ids.T, patch_count.reshape(1, -1), old_model)
+    anywhere = pl.BlockSpec(memory_space=pl.ANY)
+    return pl.pallas_call(
+        hand_on,
+        out_shape=(jax.ShapeDtypeStruct((16, 192), BF16), jax.ShapeDtypeStruct((2, 128), F32)),
+        in_specs=[anywhere, anywhere],
+        out_specs=(anywhere, anywhere),
+        scratch_shapes=[dma((2,))],
+        compiler_params=pltpu.CompilerParams(vmem_limit_bytes=60 * 1024 * 1024),
+        name="hand_on",
+    )(prob, merged)
 
 
 def solution(mesh):

time: 44.2 us -> 42.7 us (0.966)
  local copies, waits for them, and re-layouts: 2.51 us -> 0 us
  Pallas kernels: 40.8 us -> 41.9 us
    unnamed x2 -> x0, local copies, waits for them, and re-layouts: 2.51 us -> none
    pallas_call x0 -> x1, Pallas kernels: none -> 1.4 us  [shards(): pl.pallas_call(hand_on, out_shape=(jax.ShapeDtypeStruct((16, 192), BF16),...]
where the time goes in v3:
time: 42.7 us; the launch traced here: 42.5 us
  Pallas kernels  41.9 us (98%)
  between operations  0.64 us (1%)
    pallas_call x1, Pallas kernels, shards(): pl.pallas_call(kernel, out_shape=(jax.ShapeDtypeStruct((16, 192), BF16),...  40.5 us
    pallas_call x1, Pallas kernels, shards(): pl.pallas_call(hand_on, out_shape=(jax.ShapeDtypeStruct((16, 192), BF16),...  1.4 us

profile of v3, /device:TPU:1, one launch (start us, length us, event | category | flops | bytes accessed | tf_op | source)
XLA Modules:
  0.0 42.5 jit_solution(225057132141953102)
XLA Ops:
  0.6 40.5 %em_step.1 = (bf16[16,192]{1,0:T(8,128)(2,1)}, f32[2,128]{1,0:T(2,128)}) custom-call(s32[16,4096]{1,0:T(8,128)} %counts_in.1, bf16[192,4096]{1,0:T(8,128)(2,1)} %slices_in.1, s32[32,192]{1,0:T(8,128)} %bitcast.3, s32[32,192]{1,0:T(8,128)} %bitcast.4, s32[1,192]{1,0:T(1,128)} %bitcast.5, f32[2,128]{1,0:T(2,128)} %old_in.1), custom_call_target="tpu_custom_call" | custom-call | flops 2000000000 | bytes 2000000 | tf_op jit(solution)/shard_map/em_step/pallas_call | solution.py:344
  41.1 1.4 %hand_on.1 = (bf16[16,192]{1,0:T(8,128)(2,1)}, f32[2,128]{1,0:T(2,128)}) custom-call(bf16[16,192]{1,0:T(8,128)(2,1)} %get-tuple-element.4.prob_in, f32[2,128]{1,0:T(2,128)} %get-tuple-element.5.merged_in), custom_call_target="tpu_custom_call" | custom-call | tf_op jit(solution)/shard_map/hand_on/pallas_call | solution.py:391

commit v4 on v3

--- a/solution.py
+++ b/solution.py
@@ -312,7 +312,7 @@
         bsd[k] = jnp.where(sub8 < 2, tile, line)
     b_copies = [
         pltpu.make_async_remote_copy(
-            bsd.at[d], br.at[d - 1], b_send.at[d - 1], b_recv.at[d - 1],
+            bsd.at[d, 0:4], br.at[d - 1, 0:4], b_send.at[d - 1], b_recv.at[d - 1],
             device_id=place(x, (y + core * d) % YN, (z + swap * d) % ZN, core),
         )
         for d in FAR8
@@ -331,12 +331,9 @@
         copy.wait_send()
 
 
-def hand_on(prob_in, merged_in, prob_out, merged_out, sem):
-    copies = [pltpu.make_async_copy(prob_in, prob_out, sem.at[0]), pltpu.make_async_copy(merged_in, merged_out, sem.at[1])]
-    for copy in copies:
-        copy.start()
-    for copy in copies:
-        copy.wait()
+def hand_on(prob_in, merged_in, prob_out, merged_out):
+    prob_out[...] = prob_in[...]
+    merged_out[...] = merged_in[...]
 
 
 def shards(photon_counts, slices, owner_ids, tile_ids, patch_count, old_model):
@@ -387,13 +384,12 @@
         cost_estimate=pl.CostEstimate(flops=2 * 10**9, bytes_accessed=2 * 10**6, transcendentals=10**6),
         name="em_step",
     )(photon_counts, slices, owner_ids.T, tile_ids.T, patch_count.reshape(1, -1), old_model)
-    anywhere = pl.BlockSpec(memory_space=pl.ANY)
+    vmem = pl.BlockSpec(memory_space=pltpu.VMEM)
     return pl.pallas_call(
         hand_on,
         out_shape=(jax.ShapeDtypeStruct((16, 192), BF16), jax.ShapeDtypeStruct((2, 128), F32)),
-        in_specs=[anywhere, anywhere],
-        out_specs=(anywhere, anywhere),
-        scratch_shapes=[dma((2,))],
+        in_specs=[vmem, vmem],
+        out_specs=(vmem, vmem),
         compiler_params=pltpu.CompilerParams(vmem_limit_bytes=60 * 1024 * 1024),
         name="hand_on",
     )(prob, merged)

time: 42.7 us -> 42.6 us (level)
  no operation moved by 1% of the time
where the time goes in v4:
time: 42.6 us; the launch traced here: 42.4 us
  Pallas kernels  41.7 us (98%)
  between operations  0.64 us (2%)
    pallas_call x1, Pallas kernels, shards(): pl.pallas_call(kernel, out_shape=(jax.ShapeDtypeStruct((16, 192), BF16),...  40.4 us
    pallas_call x1, Pallas kernels, shards(): pl.pallas_call(hand_on, out_shape=(jax.ShapeDtypeStruct((16, 192), BF16),...  1.3 us

profile of v4, /device:TPU:1, one launch (start us, length us, event | category | flops | bytes accessed | tf_op | source)
XLA Modules:
  0.0 42.4 jit_solution(2251300817058447883)
XLA Ops:
  0.6 40.4 %em_step.1 = (bf16[16,192]{1,0:T(8,128)(2,1)}, f32[2,128]{1,0:T(2,128)}) custom-call(s32[16,4096]{1,0:T(8,128)} %counts_in.1, bf16[192,4096]{1,0:T(8,128)(2,1)} %slices_in.1, s32[32,192]{1,0:T(8,128)} %bitcast.3, s32[32,192]{1,0:T(8,128)} %bitcast.4, s32[1,192]{1,0:T(1,128)} %bitcast.5, f32[2,128]{1,0:T(2,128)} %old_in.1), custom_call_target="tpu_custom_call" | custom-call | flops 2000000000 | bytes 2000000 | tf_op jit(solution)/shard_map/em_step/pallas_call | solution.py:341
  41.1 1.3 %hand_on.1 = (bf16[16,192]{1,0:T(8,128)(2,1)}, f32[2,128]{1,0:T(2,128)}) custom-call(bf16[16,192]{1,0:T(8,128)(2,1)} %get-tuple-element.4.prob_in, f32[2,128]{1,0:T(2,128)} %get-tuple-element.5.merged_in), custom_call_target="tpu_custom_call" | custom-call | tf_op jit(solution)/shard_map/hand_on/pallas_call | solution.py:388

commit v5 on v3

--- a/solution.py
+++ b/solution.py
@@ -69,9 +69,6 @@
         pltpu.make_async_copy(count_in, pc_v, loc_sem.at[7]),
         pltpu.make_async_copy(old_in, old_v, loc_sem.at[8]),
     ]
-    for copy in locals_:
-        copy.start()
-
     barrier = pltpu.get_barrier_semaphore()
     for d in FAR8:
         pl.semaphore_signal(barrier, inc=1, device_id=place(x, (y + core * d) % YN, (z + swap * d) % ZN, core))
@@ -80,6 +77,9 @@
     for d in FAR4[:3]:
         pl.semaphore_signal(barrier, inc=1, device_id=place((x + d) % XN, y, z, swap))
     pl.semaphore_signal(barrier, inc=1, device_id=place(x, y, z, swap))
+
+    for copy in locals_:
+        copy.start()
 
     locals_[0].wait()
     fit = jnp.zeros((16, 192), F32)

time: 42.7 us -> 42.7 us (level)
  no operation moved by 1% of the time
where the time goes in v5:
time: 42.7 us; the launch traced here: 42.5 us
  Pallas kernels  41.9 us (98%)
  between operations  0.64 us (1%)
    pallas_call x1, Pallas kernels, shards(): pl.pallas_call(kernel, out_shape=(jax.ShapeDtypeStruct((16, 192), BF16),...  40.5 us
    pallas_call x1, Pallas kernels, shards(): pl.pallas_call(hand_on, out_shape=(jax.ShapeDtypeStruct((16, 192), BF16),...  1.4 us

profile of v5, /device:TPU:1, one launch (start us, length us, event | category | flops | bytes accessed | tf_op | source)
XLA Modules:
  0.0 42.5 jit_solution(7923655281840496236)
XLA Ops:
  0.6 40.5 %em_step.1 = (bf16[16,192]{1,0:T(8,128)(2,1)}, f32[2,128]{1,0:T(2,128)}) custom-call(s32[16,4096]{1,0:T(8,128)} %counts_in.1, bf16[192,4096]{1,0:T(8,128)(2,1)} %slices_in.1, s32[32,192]{1,0:T(8,128)} %bitcast.3, s32[32,192]{1,0:T(8,128)} %bitcast.4, s32[1,192]{1,0:T(1,128)} %bitcast.5, f32[2,128]{1,0:T(2,128)} %old_in.1), custom_call_target="tpu_custom_call" | custom-call | flops 2000000000 | bytes 2000000 | tf_op jit(solution)/shard_map/em_step/pallas_call | solution.py:344
  41.1 1.4 %hand_on.1 = (bf16[16,192]{1,0:T(8,128)(2,1)}, f32[2,128]{1,0:T(2,128)}) custom-call(bf16[16,192]{1,0:T(8,128)(2,1)} %get-tuple-element.4.prob_in, f32[2,128]{1,0:T(2,128)} %get-tuple-element.5.merged_in), custom_call_target="tpu_custom_call" | custom-call | tf_op jit(solution)/shard_map/hand_on/pallas_call | solution.py:391
